TPU v7x, 128 devices: a whole 4x4x4 slice. The times are simulated.
128 devices in a mesh: grp: 4 (over x_hi, core), tile: 32 (over z, y, x_lo).
Axes of the slice: x: 4 (x_hi: 2, x_lo: 2; x = x_hi * 2 + x_lo), y: 4, z: 4, core: 2. Of those that a mesh axis runs over, the one named last changes fastest.
Arguments:
- object_tile: float32 [2048, 2, 512], P('tile'), may hold values from -5 to 5
- probe: float32 [8, 2, 256, 256], replicated, may hold values from -5 to 5
- offsets: int32 [256, 2], P(('grp', 'tile')), may hold values from 0 to 1792, as said below
- frame_ids: int32 [256], P(('grp', 'tile')), may hold values from 0 to 1, as said below
- frames: float32 [256, 256, 256], P(('grp', 'tile')), may hold values from 0.2 to 3
Outputs:
- updated: float32 [2048, 2, 512], P('tile')
Inputs may be any that keep to these rules, and one draw needn't show every extreme that they name: Both offsets of a position are multiples of 32; the row offset is at most 1792 and the column offset at most 256, nodes of a regular grid of 57 x 9; the first position sits at the last node in both directions and the second at the anchor. `frame_ids`: in each aligned block of 2 positions the ids are a permutation of 0 to 1.
All inputs are finite; a program needn't handle non-finite values.
Results may differ from a plain program's by a relative error of at most 0.0014.
Values sent between devices are 32-bit elements; how exact they have to be, the bound alone decides.
A program may use at most 128 MiB of HBM per device.

v0:
```python
import functools

import jax
import jax.numpy as jnp
import ml_dtypes
import numpy as np
from jax import lax
from jax.experimental import pallas as pl
from jax.experimental.pallas import tpu as pltpu
from jax.sharding import PartitionSpec as P

MESH = pl.DeviceIdType.MESH
BF16 = jnp.bfloat16
F32 = jnp.float32
VMEM_LIMIT = 60 << 20


def _weight(step):
    return sum(min(part, 4 - part) for part in step)


STEPS = sorted(
    [
        step
        for step in ((a, b, c) for a in range(4) for b in range(4) for c in range(4))
        if _weight(step) < 3
    ],
    key=_weight,
) + [
    (2, 1, 0),
    (2, 3, 0),
    (0, 2, 1),
    (0, 2, 3),
    (1, 0, 2),
    (3, 0, 2),
    (1, 1, 1),
    (1, 3, 3),
    (3, 1, 3),
    (3, 3, 1),
]
ALL_STEPS = sorted(
    ((a, b, c) for a in range(4) for b in range(4) for c in range(4)), key=_weight, reverse=True
)[:-1]
FAR_FIRST = sorted(range(1, 32), key=lambda k: _weight(STEPS[k]), reverse=True)


class Place:
    def __init__(self):
        grp = lax.axis_index("grp")
        tile = lax.axis_index("tile")
        self.grp, self.tile = grp, tile
        self.core = lax.rem(grp, 2)
        self.x = lax.div(grp, 2) * 2 + lax.rem(tile, 2)
        self.y = lax.rem(lax.div(tile, 2), 4)
        self.z = lax.div(tile, 8)
        self.known = {}

    def once(self, name, make):
        if name not in self.known:
            self.known[name] = make()
        return self.known[name]

    def at(self, axis, by):
        by %= 4
        return self.once((axis, by), lambda: lax.rem(getattr(self, axis) + by, 4) if by else getattr(self, axis))

    def half(self, dx):
        return self.once(("half", dx % 4), lambda: lax.div(self.at("x", dx), 2) * 2)

    def tile_at(self, dx, dy, dz):
        plane = self.once(("plane", dx % 4, dy % 4), lambda: self.at("y", dy) * 2 + lax.rem(self.at("x", dx), 2))
        return self.once(("z8", dz % 4), lambda: self.at("z", dz) * 8) + plane

    def device(self, step, sign=1, other=0):
        dx, dy, dz = (sign * by for by in step)
        grp = self.once(("grp", dx % 4, other), lambda: self.half(dx) + (1 - self.core if other else self.core))
        return grp, self.tile_at(dx, dy, dz)

    def twin(self):
        return self.half(0) + 1 - self.core, self.tile

    def class_at(self, dx, dy, dz):
        near = self.once(
            ("near", dx % 4, dy % 4),
            lambda: lax.rem(self.at("x", dx), 2) * 16 + lax.rem(self.at("y", dy) + self.half(dx), 4) * 4,
        )
        return near + self.once(("deep", dx % 4, dz % 4), lambda: lax.rem(self.at("z", dz) + self.half(dx), 4))


def enter(place):
    barrier = pltpu.get_barrier_semaphore()
    for to in row_partners(place):
        pl.semaphore_signal(barrier, inc=1, device_id=to[:2], device_id_type=MESH)
    odd = lax.rem(place.tile, 2)
    beside = [step for step in STEPS if step[0] == 2]
    for step in beside:
        pl.semaphore_signal(barrier, inc=1, device_id=place.device(step, -1), device_id_type=MESH)
    ups = [step for step in STEPS if step[0] == 1]
    downs = [step for step in STEPS if step[0] == 3]
    assert len(ups) == len(downs)
    for up, down in zip(ups, downs):
        grp_a, tile_a = place.device(up, -1)
        grp_b, tile_b = place.device(down, -1)
        to = (grp_a + odd * (grp_b - grp_a), tile_a + odd * (tile_b - tile_a))
        pl.semaphore_signal(barrier, inc=1, device_id=to, device_id_type=MESH)
    pl.semaphore_signal(barrier, inc=1, device_id=place.twin(), device_id_type=MESH)
    pl.semaphore_wait(barrier, 31 + len(beside) + len(ups) + 1)


def row_partners(place):
    across = lax.rem(place.tile + 1, 2) - lax.rem(place.tile, 2)
    partners = []
    for dx, dy, dz in sorted(
        ((a, b, c) for a in range(2) for b in range(4) for c in range(4)), key=_weight, reverse=True
    )[:-1]:
        plane = place.tile_at(0, dy, dz)
        cls = place.class_at(0, dy, dz)
        partners.append((place.grp, plane + dx * across, cls + 16 * dx * across))
    return partners


def send(source, target, sems, to):
    copy = pltpu.make_async_remote_copy(
        src_ref=source,
        dst_ref=target,
        send_sem=sems.at[0],
        recv_sem=sems.at[1],
        device_id=to,
        device_id_type=MESH,
    )
    copy.start()


def arrived(ref, sems, which):
    pltpu.make_async_copy(ref, ref, sems.at[which]).wait()


def lanes_of(shape):
    return lax.broadcasted_iota(jnp.int32, shape, len(shape) - 1)


def tables():
    line = np.arange(256)
    angle = 2.0 * np.pi / 256 * (line[:, None] * line[None, :] % 256)
    re = (np.cos(angle) / 16).astype(ml_dtypes.bfloat16)
    im = (-np.sin(angle) / 16).astype(ml_dtypes.bfloat16)

    def real_form(table_re, table_im, left):
        if left:
            return np.block([[table_re, -table_im], [table_im, table_re]])
        return np.block([[table_re, table_im], [-table_im, table_re]])

    made = []
    for odd in range(2):
        made.append(real_form(re[odd::2, :128], im[odd::2, :128], True))
    for odd in range(2):
        made.append(real_form(re[:128, odd::2], im[:128, odd::2], False))
    for odd in range(2):
        made.append(real_form(re[:128, odd::2], -im[:128, odd::2], True))
    for odd in range(2):
        made.append(real_form(re[odd::2, :128], -im[odd::2, :128], False))
    order = np.zeros((256, 256), ml_dtypes.bfloat16)
    order[np.concatenate([line[0::2], line[1::2]]), line] = 1
    made.append(order)
    return np.stack([table.astype(ml_dtypes.bfloat16) for table in made])


def dot(a, b):
    return jnp.dot(a, b, preferred_element_type=F32)


def rows2(a, b):
    return jnp.concatenate([a, b], axis=0)


def cols2(a, b):
    return jnp.concatenate([a, b], axis=1)


def forward(obj, probe, table, far, power, between):
    gained = [0.0, 0.0]
    for mode in range(8):
        probe_re = probe[mode, 0]
        probe_im = probe[mode, 1]
        obj_re = obj[0]
        obj_im = obj[1]
        exit_re = probe_re * obj_re - probe_im * obj_im
        exit_im = probe_re * obj_im + probe_im * obj_re
        both = rows2(exit_re[:128] + exit_re[128:], exit_im[:128] + exit_im[128:]).astype(BF16)
        less = rows2(exit_re[:128] - exit_re[128:], exit_im[:128] - exit_im[128:]).astype(BF16)
        sums = []
        lesses = []
        for half in (dot(table[0], both), dot(table[1], less)):
            re, im = half[:128], half[128:]
            sums.append(cols2(re[:, :128] + re[:, 128:], im[:, :128] + im[:, 128:]))
            lesses.append(cols2(re[:, :128] - re[:, 128:], im[:, :128] - im[:, 128:]))
        far_even = dot(rows2(*sums).astype(BF16), table[2])
        far_odd = dot(rows2(*lesses).astype(BF16), table[3])
        far[mode, 0] = far_even
        far[mode, 1] = far_odd
        for odd, wave in enumerate((far_even, far_odd)):
            re, im = wave[:, :128], wave[:, 128:]
            gained[odd] += re * re + im * im
        between(mode)
    for odd in range(2):
        power[:, odd * 128 : odd * 128 + 128] = gained[odd]


def backward(probe, table, far, weight, grad):
    weight_even = weight[:, :128]
    weight_odd = weight[:, 128:]
    gained = [0.0, 0.0]
    for mode in range(8):
        probe_re = probe[mode, 0]
        probe_im = probe[mode, 1]
        even = far[mode, 0]
        odd = far[mode, 1]
        diff_re = cols2(even[:, :128] * weight_even, odd[:, :128] * weight_odd).astype(BF16)
        diff_im = cols2(even[:, 128:] * weight_even, odd[:, 128:] * weight_odd).astype(BF16)
        back_even = dot(table[4], rows2(diff_re[:128], diff_im[:128]))
        back_odd = dot(table[5], rows2(diff_re[128:], diff_im[128:]))
        both = back_even + back_odd
        less = back_even - back_odd
        back_re = rows2(both[:128], less[:128]).astype(BF16)
        back_im = rows2(both[128:], less[128:]).astype(BF16)
        chi_even = dot(cols2(back_re[:, :128], back_im[:, :128]), table[6])
        chi_odd = dot(cols2(back_re[:, 128:], back_im[:, 128:]), table[7])
        both = chi_even + chi_odd
        less = chi_even - chi_odd
        chi_re = cols2(both[:, :128], less[:, :128])
        chi_im = cols2(both[:, 128:], less[:, 128:])
        gained[0] += probe_re * chi_re + probe_im * chi_im
        gained[1] += probe_re * chi_im - probe_im * chi_re
    for c in range(2):
        grad[c] = gained[c]


def detector_roots(frames, frame, columns, table, root):
    for h in range(2):
        columns[h] = frames[frame, :, 128 * h : 128 * h + 128]
    value = jnp.sqrt(
        rows2(*[cols2(*[columns[h, pl.ds(odd, 128, stride=2), :] for h in range(2)]) for odd in range(2)])
    )
    first = value.astype(BF16)
    rest = value - first.astype(F32)
    second = rest.astype(BF16)
    third = (rest - second.astype(F32)).astype(BF16)
    order = table[8]
    root[...] = dot(first, order) + dot(second, order) + dot(third, order)


def kernel(
    obj_hbm,
    probe_hbm,
    frames_hbm,
    table_hbm,
    off_hbm,
    ids_hbm,
    out_ref,
    off_ref,
    ids_ref,
    tile_rows,
    probe,
    frames,
    table,
    own,
    theirs,
    mine,
    offs,
    listed,
    places,
    held,
    shifted,
    stage,
    patch_a,
    patch_b,
    obj,
    columns,
    roots,
    far,
    power,
    weight,
    grad,
    turned,
    terms,
    recv,
    counts,
    counts_in,
    totals,
    light4,
    lit,
    under,
    hits,
    split,
    result,
    ready,
    rows_in,
    load_sems,
    own_sems,
    off_sems,
    row_sems,
    patch_sems,
    term_sems,
    count_sems,
    last_sems,
    out_sems,
):
    place = Place()
    core, tile = place.core, place.tile
    my_class = place.class_at(0, 0, 0)
    cores = (core, 1 - core)
    twin = place.twin()
    patches = (patch_a, patch_b)
    loads = [
        pltpu.make_async_copy(source, target, load_sems.at[i])
        for i, (source, target) in enumerate(
            (
                (obj_hbm, tile_rows),
                (off_hbm, off_ref),
                (ids_hbm, ids_ref),
                (probe_hbm, probe),
                (table_hbm, table),
                (frames_hbm, frames),
            )
        )
    ]
    for load in loads:
        load.start()

    loads[1].wait()
    lane = lanes_of((1, 128))
    nodes = [(off_ref[p, 1] // 32) * 128 + off_ref[p, 0] // 32 for p in range(2)]
    own[...] = jnp.where(lane // 2 % 2 == core, jnp.where(lane % 2 == 0, nodes[0], nodes[1]), 0)
    enter(place)
    send(own, theirs, own_sems, twin)
    loads[0].wait()
    for grp, other, cls in row_partners(place):
        send(tile_rows.at[:, cls], held.at[pl.ds(2 * tile, 2)], row_sems, (grp, other))
    arrived(theirs, own_sems, 1)
    mine[0] = own[...] + theirs[...]
    for k in FAR_FIRST:
        send(mine.at[0], offs.at[k], off_sems, place.device(STEPS[k]))
    offs[0] = mine[0]
    held[pl.ds(2 * tile, 2)] = tile_rows[:, my_class]

    for load in loads[2:]:
        load.wait()

    def add_light(m, total):
        return total + probe[m, 0] * probe[m, 0] + probe[m, 1] * probe[m, 1]

    light = cols2(lax.fori_loop(0, 8, add_light, jnp.zeros((256, 256), F32)), jnp.zeros((256, 128), F32))
    for s in range(4):
        light4[s] = light if s == 0 else pltpu.roll(light, 32 * s, 1)
    for p in range(2):
        detector_roots(frames, ids_ref[p], columns, table, roots.at[p])
    for j in range(4):
        lit[j] = jnp.zeros((32, 128), F32)

    arrived(offs.at[pl.ds(1, 31)], off_sems, 1)
    packed = jnp.zeros((1, 128), jnp.int32)
    for k in range(32):
        packed = jnp.where(lane // 4 == k, offs[k], packed)
    listed[...] = packed
    copy = pltpu.make_async_copy(listed, places, load_sems.at[6])
    copy.start()
    arrived(held.at[pl.ds(0, 62)], row_sems, 1)
    copy.wait()
    for c in range(2):
        line = jnp.concatenate(
            [held.reshape(512, 128)[pl.ds(2 * q + c, 64, stride=8), :] for q in range(4)], axis=1
        )
        for s in range(4):
            moved_line = line if s == 0 else pltpu.roll(line, 512 - 32 * s, 1)
            for q in range(4):
                shifted[s, c, q] = moved_line[:, 128 * q : 128 * q + 128]

    def give_rows(p):
        for k in FAR_FIRST + [0]:
            value = places[0, 4 * k + 2 * cores[1 if k else 0] + p]
            a = value & 127
            b = value >> 7
            q = b >> 2
            s = b & 3
            for c in range(2):
                for h in range(2):
                    rows = shifted[s, c, q + h, pl.ds(a, 8), :]
                    if k:
                        stage[p, k, c, h] = rows
                    else:
                        patches[p][my_class, c, h] = rows
            if k:
                send(
                    stage.at[p, k],
                    patches[p].at[my_class],
                    patch_sems.at[p],
                    place.device(STEPS[k], -1, 1),
                )

    give_rows(0)

    for p in range(2):
        parts = []
        for u in range(4):
            part = jnp.zeros((1, 128), jnp.int32)
            for kk in range(16):
                part = jnp.where(lane // 8 == kk, places[0, 4 * (16 * (u % 2) + kk) + 2 * cores[u // 2] + p], part)
            parts.append(part)
        key = jnp.concatenate(parts, axis=1)
        step = lanes_of((1, 512))
        goal = (key >> 9) * 32 + (((key & 127) + 1 - core) >> 1) + step % 4
        rows = lax.broadcasted_iota(jnp.int32, (128, 512), 0)
        hits[p, 0] = jnp.where(rows == goal + (step // 4) % 2 * 32, 1.0, 0.0).astype(BF16)
        hits[p, 1] = jnp.where(rows == goal + 64, 1.0, 0.0).astype(BF16)
    grid_row = lax.broadcasted_iota(jnp.int32, (64, 128), 0)
    grid_col = lax.broadcasted_iota(jnp.int32, (64, 128), 1)
    found = jnp.zeros((64, 128), F32)
    for k in range(32):
        for row in range(4):
            value = places[0, 4 * k + row]
            found += jnp.where((grid_row == (value & 127)) & (grid_col == (value >> 7)), 1.0, 0.0)
    counts[...] = found
    send(counts, counts_in, count_sems, place.device((2, 2, 2)))
    give_rows(1)

    def frame(p, between):
        arrived(patches[p].at[pl.ds(0, 31)], patch_sems.at[p], 1)
        flat = patches[p].reshape(1024, 128)
        for c in range(2):
            for a in range(8):
                for h in range(2):
                    start = c * 16 + h * 8 + a
                    obj[c, 32 * a : 32 * a + 32, 128 * h : 128 * h + 128] = flat[pl.ds(start, 32, stride=32), :]
        forward(obj, probe, table, far, power, between)
        weight[...] = roots[p] / jnp.sqrt(jnp.maximum(power[...], 0.1)) - 1.0
        backward(probe, table, far, weight, grad)
        turn = off_ref[p, 1] & 127
        for c in range(2):
            rolled = pltpu.roll(grad[c], turn, 1)
            for h in range(2):
                turned[c, h] = rolled[:, 128 * h : 128 * h + 128]

    def lay_terms(p, other):
        start = ((cores[other] + off_ref[p, 0] // 32) & 1) * 32
        for i in range(32):
            for c in range(2):
                for h in range(2):
                    terms[p, other, i, c, 4 * h : 4 * h + 4] = turned[c, h, pl.ds(start + i, 4, stride=64), :]
        if not other:
            recv[p, 0] = terms[p, 0, my_class]

    def give_terms(p, some):
        for k, other in some:
            if k or other:
                send(
                    terms.at[p, other, place.class_at(*STEPS[k])],
                    recv.at[p, 32 * other + k],
                    term_sems.at[p, other],
                    place.device(STEPS[k], 1, other),
                )

    apart = [(k, 1) for k in FAR_FIRST + [0]]
    alike = [(k, 0) for k in FAR_FIRST]
    frame(0, lambda mode: None)
    lay_terms(0, 1)
    lay_terms(0, 0)
    frame(1, lambda mode: give_terms(0, (apart + alike)[8 * mode : 8 * mode + 8]))
    lay_terms(1, 1)
    give_terms(1, apart)
    lay_terms(1, 0)
    give_terms(1, alike)

    arrived(counts, count_sems, 1)
    totals[0:8] = jnp.zeros((8, 128), F32)
    totals[8:72] = counts[...] + counts_in[...]
    near = totals[pl.ds(2 * tile + core + 1, 8), :]
    for da in range(8):
        for b in range(9):
            q, s = b // 4, b % 4
            many = jnp.broadcast_to(near[7 - da : 8 - da, b : b + 1], (32, 128))
            for j in range(q, min(q + 3, 4)):
                if j - q == 2 and s == 0:
                    continue
                lit[j] += many * light4[s, 32 * da : 32 * da + 32, 128 * (j - q) : 128 * (j - q) + 128]
    for j in range(4):
        for c in range(2):
            under.reshape(256, 128)[pl.ds(2 * j + c, 32, stride=8), :] = lit[j] + 0.1

    sub = lax.broadcasted_iota(jnp.int32, (8, 128), 0)
    full_lane = lanes_of((8, 128))
    for p in range(2):
        for slot in list(range(32, 64, 2)) + list(range(0, 32, 2)):
            if slot == 32:
                arrived(recv.at[p, pl.ds(32, 32)], term_sems.at[p, 1], 1)
            if slot == 0:
                arrived(recv.at[p, pl.ds(1, 31)], term_sems.at[p, 0], 1)
            masks = []
            for d in range(2):
                turn = (places[0, 4 * ((slot + d) % 32) + 2 * cores[slot // 32] + p] >> 7) & 3
                masks.append((sub >= 4) | (full_lane >= 32 * turn))
            for c in range(2):
                pieces = [recv[p, slot + d, c] for d in range(2)]
                kept = rows2(*[jnp.where(masks[d], pieces[d], 0.0) for d in range(2)])
                wrapped = rows2(*[jnp.where(masks[d], 0.0, pieces[d]) for d in range(2)])
                for kind, piece in enumerate((kept, wrapped)):
                    high = piece.astype(BF16)
                    split[kind, 0, 8 * slot : 8 * slot + 16, 128 * c : 128 * c + 128] = high
                    split[kind, 1, 8 * slot : 8 * slot + 16, 128 * c : 128 * c + 128] = (
                        piece - high.astype(F32)
                    ).astype(BF16)
        part = 0.0
        for kind in range(2):
            part += dot(hits[p, kind], split[kind, 0]) + dot(hits[p, kind], split[kind, 1])
        if p == 0:
            result[...] = part
        else:
            result[...] += part
    for j in range(4):
        for c in range(2):
            ready.reshape(256, 128)[pl.ds(2 * j + c, 32, stride=8), :] = result[
                32 * j : 32 * j + 32, 128 * c : 128 * c + 128
            ]

    slot = place.half(0) * 16 + my_class
    for step in ALL_STEPS:
        send(ready.at[place.tile_at(*step)], rows_in.at[slot], last_sems, place.device(step))
    rows_in[slot] = ready[tile]
    arrived(rows_in.at[pl.ds(0, 63)], last_sems, 1)
    here = pl.ds(32 * core, 32)
    out_ref[here] = tile_rows[core] + (rows_in[0:32] + rows_in[32:64]) / under[...]
    send(out_ref.at[here], out_ref.at[here], out_sems, twin)
    arrived(out_ref.at[pl.ds(0, 32)], out_sems, 1)

    arrived(own, own_sems, 0)
    arrived(offs.at[pl.ds(1, 31)], off_sems, 0)
    arrived(held.at[pl.ds(0, 62)], row_sems, 0)
    for p in range(2):
        arrived(patches[p].at[pl.ds(0, 31)], patch_sems.at[p], 0)
        arrived(recv.at[p, pl.ds(1, 31)], term_sems.at[p, 0], 0)
        arrived(recv.at[p, pl.ds(32, 32)], term_sems.at[p, 1], 0)
    arrived(counts, count_sems, 0)
    arrived(rows_in.at[pl.ds(0, 63)], last_sems, 0)
    arrived(out_ref.at[pl.ds(0, 32)], out_sems, 0)


def on_device(object_tile, probe, offsets, frame_ids, frames):
    obj = object_tile.reshape(64, 2, 4, 128).transpose(0, 2, 1, 3).reshape(2, 32, 8, 128)
    hbm = pl.BlockSpec(memory_space=pltpu.HBM)
    pair = pltpu.SemaphoreType.DMA((2,))
    pairs = pltpu.SemaphoreType.DMA((2, 2))
    updated = pl.pallas_call(
        kernel,
        out_shape=pltpu.VMEM((64, 8, 128), F32),
        in_specs=[hbm] * 6,
        out_specs=pl.BlockSpec(memory_space=pltpu.VMEM),
        scratch_shapes=[
            pltpu.SMEM((2, 2), jnp.int32),
            pltpu.SMEM((2,), jnp.int32),
            pltpu.VMEM((2, 32, 8, 128), F32),
            pltpu.VMEM((8, 2, 256, 256), F32),
            pltpu.VMEM((2, 256, 256), F32),
            pltpu.VMEM((9, 256, 256), BF16),
            pltpu.VMEM((1, 128), jnp.int32),
            pltpu.VMEM((1, 128), jnp.int32),
            pltpu.VMEM((1, 1, 128), jnp.int32),
            pltpu.VMEM((32, 1, 128), jnp.int32),
            pltpu.VMEM((1, 128), jnp.int32),
            pltpu.SMEM((1, 128), jnp.int32),
            pltpu.VMEM((64, 8, 128), F32),
            pltpu.VMEM((4, 2, 4, 64, 128), F32),
            pltpu.VMEM((2, 32, 2, 2, 8, 128), F32),
            pltpu.VMEM((32, 2, 2, 8, 128), F32),
            pltpu.VMEM((32, 2, 2, 8, 128), F32),
            pltpu.VMEM((2, 256, 256), F32),
            pltpu.VMEM((2, 256, 128), F32),
            pltpu.VMEM((2, 256, 256), F32),
            pltpu.VMEM((8, 2, 256, 256), F32),
            pltpu.VMEM((256, 256), F32),
            pltpu.VMEM((256, 256), F32),
            pltpu.VMEM((2, 256, 256), F32),
            pltpu.VMEM((2, 2, 256, 128), F32),
            pltpu.VMEM((2, 2, 32, 2, 8, 128), F32),
            pltpu.VMEM((2, 64, 2, 8, 128), F32),
            pltpu.VMEM((64, 128), F32),
            pltpu.VMEM((64, 128), F32),
            pltpu.VMEM((72, 128), F32),
            pltpu.VMEM((4, 256, 384), F32),
            pltpu.VMEM((4, 32, 128), F32),
            pltpu.VMEM((32, 8, 128), F32),
            pltpu.VMEM((2, 2, 128, 512), BF16),
            pltpu.VMEM((2, 2, 512, 256), BF16),
            pltpu.VMEM((128, 256), F32),
            pltpu.VMEM((32, 8, 128), F32),
            pltpu.VMEM((64, 8, 128), F32),
            pltpu.SemaphoreType.DMA((7,)),
            pair,
            pair,
            pair,
            pairs,
            pltpu.SemaphoreType.DMA((2, 2, 2)),
            pair,
            pair,
            pair,
        ],
        compiler_params=pltpu.CompilerParams(
            collective_id=1, has_side_effects=True, vmem_limit_bytes=VMEM_LIMIT
        ),
        name="iteration",
    )(obj, probe, frames, jnp.asarray(tables()), offsets, frame_ids)
    return updated.reshape(64, 4, 2, 128).transpose(0, 2, 1, 3).reshape(64, 2, 512)


def solution(mesh):
    in_specs = (
        P("tile", None, None),
        P(),
        P(("grp", "tile"), None),
        P(("grp", "tile")),
        P(("grp", "tile"), None, None),
    )
    out_specs = P("tile", None, None)
    return jax.shard_map(
        on_device, mesh=mesh, in_specs=in_specs, out_specs=out_specs, check_vma=False
    )
```

profile of v0, /device:TPU:1, one launch (start us, length us, event | category | flops | bytes accessed | tf_op | source)
XLA Modules:
  0.0 51.1 jit_solution(537871159450777753)
XLA Ops:
  0.0 50.3 %iteration.1 = f32[64,8,128]{2,1,0:T(8,128)S(1)} custom-call(f32[2,32,8,128]{3,2,1,0:T(8,128)} %bitcast.11, f32[8,2,256,256]{3,2,1,0:T(8,128)} %probe_hbm.1, f32[2,256,256]{2,1,0:T(8,128)} %frames_hbm.1, bf16[9,256,256]{2,1,0:T(8,128)(2,1)} %constant.2.clone.table_hbm, s32[2,2]{1,0:T(2,128)} %off_hbm.1, s32[2]{0:T(128)} %ids_hbm.1), custom_call_target="tpu_custom_call" | custom-call | tf_op jit(solution)/shard_map/iteration/pallas_call | solution.py:551
  50.3 0.7 %copy.10 = f32[64,2,512]{2,1,0:T(2,128)} copy(f32[64,2,512]{2,1,0:T(2,128)S(1)} %bitcast.10) | data formatting | bytes 524288
where the time goes:
time: 51.1 us
  Pallas kernels  50.3 us (98%)
  local copies, waits for them, and re-layouts  0.71 us (1%)
    pallas_call x1, Pallas kernels, on_device(): pl.pallas_call(kernel, out_shape=pltpu.VMEM((64, 8, 128), F32), in_specs=...  50.3 us

commit v1 on v0

--- a/solution.py
+++ b/solution.py
@@ -87,7 +87,7 @@
         return near + self.once(("deep", dx % 4, dz % 4), lambda: lax.rem(self.at("z", dz) + self.half(dx), 4))
 
 
-def enter(place):
+def greet(place):
     barrier = pltpu.get_barrier_semaphore()
     for to in row_partners(place):
         pl.semaphore_signal(barrier, inc=1, device_id=to[:2], device_id_type=MESH)
@@ -104,7 +104,7 @@
         to = (grp_a + odd * (grp_b - grp_a), tile_a + odd * (tile_b - tile_a))
         pl.semaphore_signal(barrier, inc=1, device_id=to, device_id_type=MESH)
     pl.semaphore_signal(barrier, inc=1, device_id=place.twin(), device_id_type=MESH)
-    pl.semaphore_wait(barrier, 31 + len(beside) + len(ups) + 1)
+    return 31 + len(beside) + len(ups) + 1
 
 
 def row_partners(place):
@@ -324,14 +324,16 @@
             )
         )
     ]
-    for load in loads:
+    loads[0].start()
+    met = greet(place)
+    for load in loads[1:]:
         load.start()
 
     loads[1].wait()
     lane = lanes_of((1, 128))
     nodes = [(off_ref[p, 1] // 32) * 128 + off_ref[p, 0] // 32 for p in range(2)]
     own[...] = jnp.where(lane // 2 % 2 == core, jnp.where(lane % 2 == 0, nodes[0], nodes[1]), 0)
-    enter(place)
+    pl.semaphore_wait(pltpu.get_barrier_semaphore(), met)
     send(own, theirs, own_sems, twin)
     loads[0].wait()
     for grp, other, cls in row_partners(place):

time: 51.1 us -> 50.2 us (0.982)
  Pallas kernels: 50.3 us -> 49.3 us
    pallas_call x1, Pallas kernels: 50.3 us -> 49.3 us  [on_device(): pl.pallas_call(kernel, out_shape=pltpu.VMEM((64, 8, 128), F32), in_specs=...]
where the time goes in v1:
time: 50.2 us; the launch traced here: 50.1 us
  Pallas kernels  49.3 us (98%)
  local copies, waits for them, and re-layouts  0.71 us (1%)
    pallas_call x1, Pallas kernels, on_device(): pl.pallas_call(kernel, out_shape=pltpu.VMEM((64, 8, 128), F32), in_specs=...  49.3 us

profile of v1, /device:TPU:1, one launch (start us, length us, event | category | flops | bytes accessed | tf_op | source)
XLA Modules:
  0.0 50.1 jit_solution(2209317483467225644)
XLA Ops:
  0.0 49.3 %iteration.1 = f32[64,8,128]{2,1,0:T(8,128)S(1)} custom-call(f32[2,32,8,128]{3,2,1,0:T(8,128)} %bitcast.11, f32[8,2,256,256]{3,2,1,0:T(8,128)} %probe_hbm.1, f32[2,256,256]{2,1,0:T(8,128)} %frames_hbm.1, bf16[9,256,256]{2,1,0:T(8,128)(2,1)} %constant.2.clone.table_hbm, s32[2,2]{1,0:T(2,128)} %off_hbm.1, s32[2]{0:T(128)} %ids_hbm.1), custom_call_target="tpu_custom_call" | custom-call | tf_op jit(solution)/shard_map/iteration/pallas_call | solution.py:553
  49.4 0.7 %copy.10 = f32[64,2,512]{2,1,0:T(2,128)} copy(f32[64,2,512]{2,1,0:T(2,128)S(1)} %bitcast.10) | data formatting | bytes 524288
